TPU v7x, 512 devices: a whole 4x4x16 slice. The times are simulated.
512 devices in a mesh: ens: 32 (over z, x_lo), grid: 16 (over y, x_hi, core).
Axes of the slice: x: 4 (x_hi: 2, x_lo: 2; x = x_hi * 2 + x_lo), y: 4, z: 16, core: 2. Of those that a mesh axis runs over, the one named last changes fastest.
Arguments:
- hidden: bfloat16 [32, 12288, 1024], P('ens', 'grid'), may hold values from -6 to 6
- weight: bfloat16 [100, 1024], replicated, may hold values from -0.1875 to 0.1875
- bias: float32 [100], replicated, may hold values from -3 to 3
- target: float32 [100, 12288], P(None, 'grid'), may hold values from -6 to 6
- area_weight: float32 [12288], P('grid'), may hold values from 0.3 to 3
- var_weight: float32 [100], replicated, may hold values from 0.3 to 3
Outputs:
- loss: float32 [], replicated
- grad_hidden: bfloat16 [32, 12288, 1024], P('ens', 'grid')
- grad_weight: float32 [100, 1024], replicated
- grad_bias: float32 [100], replicated
All inputs are finite; a program needn't handle non-finite values.
Results may differ from a plain program's by a relative error of at most 0.013.
Values may be sent and summed in bfloat16 or wider, within the bound.
A program may use at most 64 MiB of HBM per device.

v0:
```python
import jax
import jax.numpy as jnp
from jax import lax
from jax.sharding import PartitionSpec as P

alpha_fair = 0.95
smooth = 0.3


def soft_abs(diff):
    return jnp.sqrt(diff * diff + smooth * smooth) - smooth


def soft_sign(diff):
    return diff / jnp.sqrt(diff * diff + smooth * smooth)


def body(hidden, weight, bias, target, area_weight, var_weight):
    rows = hidden[0]
    members = lax.axis_size("ens")
    points = rows.shape[0] * lax.axis_size("grid")
    width_v = weight.shape[0]
    raw = lax.dot_general(
        weight, rows, (((1,), (1,)), ((), ())), preferred_element_type=jnp.float32
    )
    pred = (raw + bias[:, None]).astype(jnp.bfloat16)
    values = pred.astype(jnp.float32)
    eps = (1.0 - alpha_fair) / members
    pair_coef = (1.0 - eps) / (members - 1)
    half_coef = (1.0 - eps) / (2.0 * members * (members - 1))
    scale = var_weight[:, None] * area_weight[None, :]
    diff = values[None] - lax.all_gather(pred[None], "ens", axis=0, tiled=True).astype(jnp.float32)
    pair_sign = jnp.sum(soft_sign(diff), axis=0)
    pair_abs = jnp.sum(soft_abs(diff), axis=0)
    member_crps = soft_abs(values - target) / members - half_coef * pair_abs
    loss_part = jnp.sum(scale * member_crps) / (points * width_v)
    grad_pred = (scale * (soft_sign(values - target) - pair_coef * pair_sign)).astype(jnp.bfloat16)
    grad_rows = lax.dot_general(
        grad_pred, weight, (((0,), (0,)), ((), ())), preferred_element_type=jnp.float32
    )
    grad_hidden = grad_rows.astype(jnp.bfloat16)[None]
    weight_part = jnp.dot(grad_pred, rows, preferred_element_type=jnp.float32) / points
    bias_part = jnp.sum(grad_pred.astype(jnp.float32), axis=1) / points
    loss, grad_bias = lax.psum((loss_part, bias_part), ("ens", "grid"))
    grad_weight = lax.psum(weight_part, ("ens", "grid"))
    return (loss, grad_hidden, grad_weight, grad_bias)


def solution(mesh):
    return jax.shard_map(
        body,
        mesh=mesh,
        in_specs=(P("ens", "grid", None), P(), P(), P(None, "grid"), P("grid"), P()),
        out_specs=(P(), P("ens", "grid", None), P(), P()),
        check_vma=False,
    )
```

profile of v0, /device:TPU:1, one launch (start us, length us, event | category | flops | bytes accessed | tf_op | source)
XLA Modules:
  0.0 634.1 jit_solution(14466720614790900323)
XLA Ops:
  7.2 0.0 copy-start
  7.2 0.0 copy-start.5
  7.2 0.0 copy-start.4
  7.2 0.0 copy-start.3
  7.2 0.0 all-gather.4.cloned.1.call-start
  7.3 1.3 copy-done
  8.6 2.2 fusion.24
  10.8 0.0 copy-start.1
  10.8 0.0 copy-start.2
  10.8 0.0 all-gather.4.cloned.1.call-update
  10.8 0.0 all-reduce.3.cloned.1.call-start
  10.9 134.7 %all-gather.4.cloned.1.call-done = bf16[32,100,768]{2,1,0:T(8,128)(2,1)} async-done(((bf16[1,100,768]{2,1,0:T(8,128)(2,1)}), bf16[32,100,768]{2,1,0:T(8,128)(2,1)}) %all-gather.4.cloned.1.call-update) | async-done | bytes 4915216 | tf_op jit(solution)/shard_map/all_gather | solution.py:32
  145.6 7.1 %fusion.6 = (f32[100,768]{1,0:T(8,128)S(1)}, f32[100,768]{1,0:T(8,128)S(1)}) fusion(bf16[32,100,768]{2,1,0:T(8,128)(2,1)} %all-gather.4.cloned.1.call-done, f32[100,768]{1,0:T(8,128)S(1)} %get-tuple-element.11), kind=kLoop, calls=%fused_computation.7 | loop fusion | flops 19507200 | bytes 5836800 | tf_op jit(solution)/shard_map/reduce_sum | solution.py:33
  152.8 0.0 copy-done.5
  152.8 0.0 copy-done.4
  152.8 0.0 copy-done.3
  152.8 0.0 copy-done.1
  152.8 0.9 convert_reduce_fusion
  153.7 1.1 fusion.12
  154.9 0.0 all-reduce.3.cloned.1.call-update
  155.6 119.2 %all-reduce = (f32[]{:T(128)}, f32[100]{0:T(128)}) all-reduce(f32[]{:T(128)S(6)} %div.29, f32[100]{0:T(128)S(1)} %broadcast_multiply_fusion), channel_id=1, replica_groups=mesh['ens'=32,'grid'=16] {'ens','grid'}, use_global_device_ids=true, to_apply=%region_2.0 | all-reduce | flops 101 | bytes 808 | tf_op jit(solution)/shard_map/psum | solution.py:44
  274.7 0.0 copy-done.2
  274.7 1.8 fusion.11
  276.5 349.0 %all-reduce.3.cloned.1.call-done = f32[100,1024]{1,0:T(8,128)} async-done(((f32[100,1024]{1,0:T(8,128)}), f32[100,1024]{1,0:T(8,128)}) %all-reduce.3.cloned.1.call-update) | async-done | bytes 409616 | tf_op jit(solution)/shard_map/psum | solution.py:45
  625.5 1.8 copy.11
  (1 shorter events, 0.0 us)
Async XLA Ops:
  7.2 1.4 copy-start
  7.2 145.6 %copy-start.5 = (f32[100]{0:T(128)S(1)}, f32[100]{0:T(128)}, u32[]{:S(2)}) copy-start(f32[100]{0:T(128)} %param.11) | copy-start | bytes 1204
  7.2 145.6 %copy-start.4 = (f32[768]{0:T(1024)S(1)}, f32[768]{0:T(1024)}, u32[]{:S(2)}) copy-start(f32[768]{0:T(1024)} %param.10) | copy-start | bytes 9220
  7.2 145.6 %copy-start.3 = (f32[100,768]{1,0:T(8,128)S(1)}, f32[100,768]{1,0:T(8,128)}, u32[]{:S(2)}) copy-start(f32[100,768]{1,0:T(8,128)} %param.9) | copy-start | bytes 921604
  7.2 138.4 %all-gather.4.cloned.1.call-start = ((), (), s32[]{:S(2)}) async-start(), calls=%async_computation.1 | async-start | bytes 5271552 | tf_op jit(solution)/shard_map/all_gather | solution.py:32
  10.8 142.0 %copy-start.1 = (bf16[100,768]{1,0:T(8,128)(2,1)S(1)}, bf16[100,768]{1,0:T(8,128)(2,1)}, u32[]{:S(2)}) copy-start(bf16[100,768]{1,0:T(8,128)(2,1)} %get-tuple-element.12) | copy-start | bytes 460804
  10.8 263.9 %copy-start.2 = (bf16[100,1024]{1,0:T(8,128)(2,1)S(1)}, bf16[100,1024]{1,0:T(8,128)(2,1)}, u32[]{:S(2)}) copy-start(bf16[100,1024]{1,0:T(8,128)(2,1)} %param.7) | copy-start | bytes 614404
  10.8 614.6 %all-reduce.3.cloned.1.call-start = ((), (), s32[]{:S(2)}) async-start(), calls=%async_computation | async-start | bytes 851968 | tf_op jit(solution)/shard_map/psum | solution.py:45
Sparse Core Ops, SparseCore 0:
  11.0 134.6 all-gather.3
  155.0 470.3 all-reduce.2
where the time goes:
time: 636 us; the launch traced here: 634 us
  waiting for transfers between devices  484 us (76%)
  blocking collectives  119 us (19%)
  between operations  14.8 us (2%)
  other arithmetic  8.06 us (1%)
    psum x1, waiting for transfers between devices, body(): grad_weight = lax.psum(weight_part, ('ens', 'grid'))  349 us
    all_gather x1, waiting for transfers between devices, body(): lax.all_gather(pred[None], 'ens', axis=0, tiled=True).astype(jnp.float32)  135 us
    psum x1, blocking collectives, body(): loss, grad_bias = lax.psum((loss_part, bias_part), ('ens', 'grid'))  119 us
  transfers between devices with their start and end apart: 2, of which 2 were waited for; matrix products, arithmetic and copies ran while one was open for 0% of the time, Pallas kernels for 0%

commit v1 on v0

v1 whole, which is shorter than its diff:
```python
import functools
import math

import jax
import jax.numpy as jnp
from jax import lax
from jax.experimental import pallas as pl
from jax.experimental.pallas import tpu as pltpu
from jax.sharding import PartitionSpec as P

alpha_fair = 0.95
smooth = 0.3
MESH = pl.DeviceIdType.MESH
F32 = jnp.float32
BF16 = jnp.bfloat16
XL = 2


class Plan:
    def __init__(self, mesh_shape, V, H, G):
        self.E, self.NG = mesh_shape["ens"], mesh_shape["grid"]
        self.V, self.H, self.G = V, H, G
        self.NZ = self.E // XL
        self.VG, self.REM = V // 16, V % 16
        self.NT, self.HC = G // 128, H // 128
        self.FOLD = 16 // self.REM
        self.RT = -(-self.NT // self.FOLD)
        self.FULL = self.VG * self.NT
        self.T = self.FULL + self.RT
        self.TAIL = self.T - self.E
        self.STEP = max(1, self.NZ // max(1, self.TAIL))
        self.PL = XL * self.NG
        self.WF = self.VG * self.HC // 2
        self.NPART = self.WF + -(-(self.REM * self.HC) // 32)
        self.ZR = 32 // self.NZ

    def rank_of(self, e):
        z, xl = e // XL, e % XL
        return jnp.where(xl == z % 2, z, self.NZ + z)

    def owner(self, r):
        z = r % self.NZ
        return z * XL + (r + r // self.NZ) % 2


def kernel(pn, hid_hbm, w_hbm, bias_hbm, tgt_hbm, area_hbm, var_hbm, gp_ref, gw_ref, x_ref,
           hid, w, bias, target, area, var, tgt, scl, varb, bcol, tmp, rem, S, R, G, B, pv, acc,
           xs, X, zx, PP, Q, zs, zr, zo, zg, U, F,
           in_sem, s_send, s_recv, g_send, b_recv, p_send, q_recv, x_send, x_recv, zx_send, zx_recv,
           z_send, z_recv, zg_send, zg_recv, u_send, f_recv):
    E, NG, NZ, VG, REM, NT, HC = pn.E, pn.NG, pn.NZ, pn.VG, pn.REM, pn.NT, pn.HC
    V, FULL, T, TAIL, NPL = pn.V, pn.FULL, pn.T, pn.TAIL, pn.PL
    e = lax.axis_index("ens")
    g = lax.axis_index("grid")
    myz, myx = e // XL, e % XL
    r = pn.rank_of(e)
    q = g * XL + myx

    def plane(k):
        return {"ens": myz * XL + k % XL, "grid": k // XL}

    def column(k):
        return {"ens": k * XL + myx}

    def landed(ref, sem):
        pltpu.make_async_copy(ref, ref, sem).wait()

    ins = [(w_hbm, w), (bias_hbm, bias), (tgt_hbm, target), (area_hbm, area), (var_hbm, var)]
    in_copies = [pltpu.make_async_copy(a, b, in_sem.at[i]) for i, (a, b) in enumerate(ins)]
    hid_copies = [
        pltpu.make_async_copy(hid_hbm.at[pl.ds(t * 128, 128)], hid.at[pl.ds(t * 128, 128)], in_sem.at[len(ins) + t])
        for t in range(NT)
    ]
    in_copies[0].start()
    in_copies[1].start()
    for c in hid_copies:
        c.start()
    for c in in_copies[2:]:
        c.start()

    barrier = pltpu.get_barrier_semaphore()

    @pl.loop(1, E)
    def _(i):
        pl.semaphore_signal(barrier, inc=1, device_id={"ens": lax.rem(e + i, E)}, device_id_type=MESH)

    @pl.loop(1, NPL)
    def _(i):
        pl.semaphore_signal(barrier, inc=1, device_id=plane(lax.rem(q + i, NPL)), device_id_type=MESH)

    in_copies[0].wait()
    in_copies[1].wait()
    varb[...] = jnp.zeros_like(varb)
    varb[:, 0:V] = jnp.broadcast_to(bias[...], (128, V))
    biasb = varb[...].T[0:V]
    rem[...] = jnp.zeros_like(rem)
    for t in range(NT):
        hid_copies[t].wait()
        raw = lax.dot_general(w[...], hid[t * 128:(t + 1) * 128], (((1,), (1,)), ((), ())), preferred_element_type=F32)
        pred = raw + biasb
        for vg in range(VG):
            S[t * VG + vg] = pred[16 * vg:16 * vg + 16].astype(BF16)
        rem[REM * t:REM * t + REM] = pred[16 * VG:V]
    for i in range(pn.RT):
        S[FULL + i] = rem[16 * i:16 * i + 16].astype(BF16)

    pl.semaphore_wait(barrier, E - 1 + NPL - 1)

    def send_tile(slot, j, rank):
        own = pn.owner(rank)

        @pl.when(own == e)
        def _():
            pltpu.make_async_copy(S.at[j], R.at[slot, e], s_recv.at[slot]).start()

        @pl.when(own != e)
        def _():
            pltpu.make_async_remote_copy(
                src_ref=S.at[j], dst_ref=R.at[slot, e], send_sem=s_send.at[slot], recv_sem=s_recv.at[slot],
                device_id={"ens": own}, device_id_type=MESH).start()

    @pl.loop(0, E)
    def _(i):
        rank = lax.rem(r + i, E)
        send_tile(0, rank, rank)

    @pl.loop(0, TAIL)
    def _(i):
        send_tile(1, E + i, i * pn.STEP)

    for c in in_copies[2:]:
        c.wait()
    varb[:, 0:V] = jnp.broadcast_to(var[...], (128, V))
    varb[...] = varb[...].T
    bcol[...] = jnp.zeros_like(bcol)

    tail_i = r // pn.STEP
    has_tail = jnp.logical_and(r % pn.STEP == 0, tail_i < TAIL)

    def prepare(slot, j):
        @pl.when(j < FULL)
        def _():
            vrow = pl.multiple_of((j % VG) * 16, 16)
            col = pl.multiple_of((j // VG) * 128, 128)
            tgt[slot] = target[pl.ds(vrow, 16), pl.ds(col, 128)]
            scl[slot] = varb[pl.ds(vrow, 16)] * area[0:1, pl.ds(col, 128)]

        for i in range(pn.RT):
            @pl.when(j == FULL + i)
            def _():
                tgt[slot] = jnp.zeros((16, 128), F32)
                scl[slot] = jnp.zeros((16, 128), F32)
                for k in range(pn.FOLD):
                    t = i * pn.FOLD + k
                    if t < NT:
                        cols = slice(128 * t, 128 * t + 128)
                        tgt[slot, REM * k:REM * k + REM] = target[16 * VG:V, cols]
                        scl[slot, REM * k:REM * k + REM] = varb[16 * VG:V] * area[0:1, cols]

    prepare(0, r)

    @pl.when(has_tail)
    def _():
        prepare(1, E + tail_i)

    members = E
    eps = (1.0 - alpha_fair) / members
    pair_coef = (1.0 - eps) / (members - 1)
    c2 = smooth * smooth
    BM = min(8, E // 2)
    NB = E // BM

    def blocks(h, i, j, total, diag):
        rows = pl.ds(h * 8, 8)
        a = [pv[i * BM + k, rows] for k in range(BM)]
        b = a if diag else [pv[j * BM + k, rows] for k in range(BM)]
        sa = [acc[i * BM + k, rows] for k in range(BM)]
        sb = sa if diag else [acc[j * BM + k, rows] for k in range(BM)]
        for m in range(BM):
            for k in range(m + 1 if diag else 0, BM):
                d = a[m] - b[k]
                qq = d * d + c2
                rs = lax.rsqrt(qq)
                s = d * rs
                total = total + qq * rs
                sa[m] = sa[m] + s
                sb[k] = sb[k] - s
        for k in range(BM):
            acc[i * BM + k, rows] = sa[k]
            if not diag:
                acc[j * BM + k, rows] = sb[k]
        return total

    def process(slot, j):
        landed(R.at[slot], s_recv.at[slot])

        @pl.loop(0, E)
        def _(m):
            pv[m] = R[slot, m].astype(F32)
            acc[m] = jnp.zeros((16, 128), F32)

        def half(h, _):
            total = lax.fori_loop(0, NB, lambda i, t: blocks(h, i, i, t, True), jnp.zeros((8, 128), F32))

            def off(k, t):
                if NB == 2:
                    return blocks(h, 0, 1, t, False)
                return blocks(h, k % 4, (k + 1 + k // 4) % 4, t, False)
            tmp[pl.ds(h * 8, 8)] = lax.fori_loop(0, NB * (NB - 1) // 2, off, total)
            return 0
        lax.fori_loop(0, 2, half, 0)
        tg, sc = tgt[slot], scl[slot]

        def finish(m, carry):
            bsum, absum = carry
            d = pv[m] - tg
            qq = d * d + c2
            rs = lax.rsqrt(qq)
            gb = (sc * (d * rs - pair_coef * acc[m])).astype(BF16)
            G[slot, m] = gb
            return bsum + gb.astype(F32), absum + qq * rs
        zero = jnp.zeros((16, 128), F32)
        bsum, absum = lax.fori_loop(0, E, finish, (zero, zero))

        @pl.loop(0, E)
        def _(i):
            m = lax.rem(e + i, E)

            @pl.when(m == e)
            def _():
                pltpu.make_async_copy(G.at[slot, m], B.at[j], b_recv).start()

            @pl.when(m != e)
            def _():
                pltpu.make_async_remote_copy(
                    src_ref=G.at[slot, m], dst_ref=B.at[j], send_sem=g_send.at[slot], recv_sem=b_recv,
                    device_id={"ens": m}, device_id_type=MESH).start()

        npair = members * (members - 1) // 2
        crps = (absum - members * smooth) / members - 2.0 * (pair_coef / (2.0 * members)) * (tmp[...] - npair * smooth)
        lossb = jnp.broadcast_to(jnp.sum(sc * crps, axis=(0, 1), keepdims=True), (8, 128))
        bcol[V + 4:V + 12] = bcol[V + 4:V + 12] + lossb
        bb = jnp.broadcast_to(jnp.sum(bsum, axis=1, keepdims=True), (16, 128))

        @pl.when(j < FULL)
        def _():
            rows = pl.ds(pl.multiple_of((j % VG) * 16, 16), 16)
            bcol[rows] = bcol[rows] + bb

        @pl.when(j >= FULL)
        def _():
            tmp[...] = bb
            fold = tmp[0:REM]
            for k in range(1, pn.FOLD):
                fold = fold + tmp[REM * k:REM * k + REM]
            bcol[16 * VG:V] = bcol[16 * VG:V] + fold

    process(0, r)

    @pl.when(has_tail)
    def _():
        process(1, E + tail_i)

    xs[...] = bcol[...].T[0:1]
    X[q] = xs[...]

    @pl.loop(1, NPL)
    def _(i):
        k = lax.rem(q + i, NPL)
        pltpu.make_async_remote_copy(
            src_ref=xs, dst_ref=X.at[q], send_sem=x_send, recv_sem=x_recv, device_id=plane(k), device_id_type=MESH).start()

    landed(B, b_recv)
    for t in range(NT):
        for vg in range(VG):
            gp_ref[16 * vg:16 * vg + 16, 128 * t:128 * t + 128] = B[t * VG + vg]
    for i in range(pn.RT):
        rem[16 * i:16 * i + 16] = B[FULL + i].astype(F32)
    for t in range(NT):
        gp_ref[16 * VG:V, 128 * t:128 * t + 128] = rem[REM * t:REM * t + REM].astype(BF16)

    CW = 256
    for cc in range(pn.H // CW):
        part = lax.dot_general(gp_ref[...], hid[:, cc * CW:(cc + 1) * CW], (((1,), (0,)), ((), ())), preferred_element_type=F32)
        for c2_ in range(CW // 128):
            c = cc * (CW // 128) + c2_
            cols = slice(128 * c2_, 128 * c2_ + 128)
            for vg in range(VG):
                n = c * VG + vg
                PP[n // 2, n % 2] = part[16 * vg:16 * vg + 16, cols].astype(BF16)
            rem[REM * c:REM * c + REM] = part[16 * VG:V, cols]
    for i in range(2):
        PP[pn.WF, i] = rem[16 * i:16 * i + 16].astype(BF16)

    @pl.loop(0, NPL)
    def _(i):
        k = lax.rem(q + i, NPL)

        @pl.when(jnp.logical_and(k < pn.NPART, k == q))
        def _():
            pltpu.make_async_copy(PP.at[k], Q.at[q], q_recv).start()

        @pl.when(jnp.logical_and(k < pn.NPART, k != q))
        def _():
            pltpu.make_async_remote_copy(
                src_ref=PP.at[k], dst_ref=Q.at[q], send_sem=p_send, recv_sem=q_recv,
                device_id=plane(k), device_id_type=MESH).start()

    landed(X.at[pl.ds(0, NPL - 1)], x_recv)
    zx[myz] = lax.fori_loop(1, NPL, lambda i, s: s + X[i], X[0])

    @pl.loop(1, NZ)
    def _(i):
        k = lax.rem(myz + i, NZ)
        pltpu.make_async_remote_copy(
            src_ref=zx.at[myz], dst_ref=zx.at[myz], send_sem=zx_send, recv_sem=zx_recv,
            device_id=column(k), device_id_type=MESH).start()

    points = pn.G * NG

    @pl.when(q < pn.NPART)
    def _():
        landed(Q, q_recv)
        total = lax.fori_loop(0, NPL, lambda i, s: s + Q[i].astype(F32), jnp.zeros((2, 16, 128), F32))
        for i in range(2):
            rem[16 * i:16 * i + 16] = total[i]
        for k in range(NZ):
            zs[k] = rem[pn.ZR * k:pn.ZR * k + pn.ZR]
        zr[myz] = zs[myz]

        @pl.loop(1, NZ)
        def _(i):
            k = lax.rem(myz + i, NZ)
            pltpu.make_async_remote_copy(
                src_ref=zs.at[k], dst_ref=zr.at[myz], send_sem=z_send, recv_sem=z_recv,
                device_id=column(k), device_id_type=MESH).start()
        landed(zr.at[pl.ds(0, NZ - 1)], z_recv)
        zo[...] = lax.fori_loop(0, NZ, lambda i, s: s + zr[i], jnp.zeros((pn.ZR, 128), F32)) * (1.0 / points)
        zg[myz] = zo[...]

        @pl.loop(1, NZ)
        def _(i):
            k = lax.rem(myz + i, NZ)
            pltpu.make_async_remote_copy(
                src_ref=zo, dst_ref=zg.at[myz], send_sem=zg_send, recv_sem=zg_recv,
                device_id=column(k), device_id_type=MESH).start()
        landed(zg.at[pl.ds(0, NZ - 1)], zg_recv)
        for k in range(NZ):
            rem[pn.ZR * k:pn.ZR * k + pn.ZR] = zg[k]
        for i in range(2):
            U[i] = rem[16 * i:16 * i + 16].astype(BF16)

        @pl.loop(0, NPL)
        def _(i):
            k = lax.rem(q + i, NPL)

            @pl.when(k == q)
            def _():
                pltpu.make_async_copy(U, F.at[q], f_recv).start()

            @pl.when(k != q)
            def _():
                pltpu.make_async_remote_copy(
                    src_ref=U, dst_ref=F.at[q], send_sem=u_send, recv_sem=f_recv,
                    device_id=plane(k), device_id_type=MESH).start()

    landed(zx.at[pl.ds(0, NZ - 1)], zx_recv)
    x_ref[...] = lax.fori_loop(0, NZ, lambda i, s: s + zx[i], jnp.zeros((1, 128), F32)) * (1.0 / points)

    landed(F, f_recv)
    for c in range(HC):
        for vg in range(VG):
            n = c * VG + vg
            gw_ref[16 * vg:16 * vg + 16, 128 * c:128 * c + 128] = F[n // 2, n % 2].astype(F32)
    for i in range(2):
        rem[16 * i:16 * i + 16] = F[pn.WF, i].astype(F32)
    for c in range(HC):
        gw_ref[16 * VG:V, 128 * c:128 * c + 128] = rem[REM * c:REM * c + REM]

    landed(S.at[pl.ds(0, E - 1)], s_send.at[0])
    landed(G.at[0, pl.ds(0, E - 1)], g_send.at[0])
    landed(X.at[pl.ds(0, NPL - 1)], x_send)
    landed(zx.at[pl.ds(0, NZ - 1)], zx_send)

    @pl.when(has_tail)
    def _():
        landed(S.at[pl.ds(0, TAIL - 1)], s_send.at[1])
        landed(G.at[1, pl.ds(0, E - 1)], g_send.at[1])

    @pl.when(jnp.logical_not(has_tail))
    def _():
        landed(S.at[pl.ds(0, TAIL)], s_send.at[1])

    @pl.when(q < pn.NPART)
    def _():
        landed(PP.at[pl.ds(0, pn.NPART - 1)], p_send)
        landed(zs.at[pl.ds(0, NZ - 1)], z_send)
        landed(zs.at[pl.ds(0, NZ - 1)], zg_send)
        landed(Q.at[pl.ds(0, NPL - 1)], u_send)

    @pl.when(q >= pn.NPART)
    def _():
        landed(PP, p_send)


def body(mesh_shape, hidden, weight, bias, target, area_weight, var_weight):
    rows = hidden[0]
    V, H = weight.shape
    G = rows.shape[0]
    pn = Plan(mesh_shape, V, H, G)
    E, NZ = pn.E, pn.NZ
    dma = pltpu.SemaphoreType.DMA
    gp, gw, x = pl.pallas_call(
        functools.partial(kernel, pn),
        out_shape=(
            jax.ShapeDtypeStruct((V, G), BF16),
            jax.ShapeDtypeStruct((V, H), F32),
            jax.ShapeDtypeStruct((1, 128), F32),
        ),
        in_specs=[pl.BlockSpec(memory_space=pl.ANY)] * 6,
        out_specs=(pl.BlockSpec(memory_space=pltpu.VMEM),) * 3,
        scratch_shapes=[
            pltpu.VMEM((G, H), BF16),
            pltpu.VMEM((V, H), BF16),
            pltpu.VMEM((1, V), F32),
            pltpu.VMEM((V, G), F32),
            pltpu.VMEM((1, G), F32),
            pltpu.VMEM((1, V), F32),
            pltpu.VMEM((2, 16, 128), F32),
            pltpu.VMEM((2, 16, 128), F32),
            pltpu.VMEM((128, 128), F32),
            pltpu.VMEM((128, 128), F32),
            pltpu.VMEM((16, 128), F32),
            pltpu.VMEM((32, 128), F32),
            pltpu.VMEM((pn.T, 16, 128), BF16),
            pltpu.VMEM((2, E, 16, 128), BF16),
            pltpu.VMEM((2, E, 16, 128), BF16),
            pltpu.VMEM((pn.T, 16, 128), BF16),
            pltpu.VMEM((E, 16, 128), F32),
            pltpu.VMEM((E, 16, 128), F32),
            pltpu.VMEM((1, 128), F32),
            pltpu.VMEM((pn.PL, 1, 128), F32),
            pltpu.VMEM((NZ, 1, 128), F32),
            pltpu.VMEM((pn.NPART, 2, 16, 128), BF16),
            pltpu.VMEM((pn.PL, 2, 16, 128), BF16),
            pltpu.VMEM((NZ, pn.ZR, 128), F32),
            pltpu.VMEM((NZ, pn.ZR, 128), F32),
            pltpu.VMEM((pn.ZR, 128), F32),
            pltpu.VMEM((NZ, pn.ZR, 128), F32),
            pltpu.VMEM((2, 16, 128), BF16),
            pltpu.VMEM((pn.NPART, 2, 16, 128), BF16),
            dma((5 + pn.NT,)),
            dma((2,)),
            dma((2,)),
            dma((2,)),
            dma, dma, dma, dma, dma, dma, dma, dma, dma, dma, dma, dma, dma,
        ],
        compiler_params=pltpu.CompilerParams(
            collective_id=0, has_side_effects=True, vmem_limit_bytes=32 * 1024 * 1024
        ),
        cost_estimate=pl.CostEstimate(flops=4 * V * G * H, bytes_accessed=2 * G * H, transcendentals=V * G * 16),
    )(rows, weight, bias[None], target, area_weight[None], var_weight[None])
    grad_rows = lax.dot_general(gp, weight, (((0,), (0,)), ((), ())), preferred_element_type=F32)
    loss = x[0, V + 4] / V
    grad_bias = x[0, :V]
    return (loss, grad_rows.astype(BF16)[None], gw, grad_bias)


def solution(mesh):
    return jax.shard_map(
        functools.partial(body, dict(mesh.shape)),
        mesh=mesh,
        in_specs=(P("ens", "grid", None), P(), P(), P(None, "grid"), P("grid"), P()),
        out_specs=(P(), P("ens", "grid", None), P(), P()),
        check_vma=False,
    )
```

time: 636 us -> 83.2 us (0.13)
  waiting for transfers between devices: 484 us -> 0 us
  blocking collectives: 119 us -> 0 us
  Pallas kernels: 0 us -> 71.5 us
  between operations: 14.8 us -> 2.43 us
  other arithmetic: 8.06 us -> 0 us
    psum x1 -> x0, waiting for transfers between devices: 349 us -> none  [body(): grad_weight = lax.psum(weight_part, ('ens', 'grid'))]
    all_gather x1 -> x0, waiting for transfers between devices: 135 us -> none  [body(): lax.all_gather(pred[None], 'ens', axis=0, tiled=True).astype(jnp.float32)]
    psum x1 -> x0, blocking collectives: 119 us -> none  [body(): loss, grad_bias = lax.psum((loss_part, bias_part), ('ens', 'grid'))]
    pallas_call x0 -> x1, Pallas kernels: none -> 71.5 us  [body(): pl.pallas_call(functools.partial(kernel, pn), out_shape=(jax.ShapeDtypeSt...]
    reduce_sum x2 -> x0, other arithmetic: 8.06 us -> none  [the longest x1 7.14 us: body(): pair_sign = jnp.sum(soft_sign(diff), axis=0)]
  transfers between devices with their start and end apart: 2 -> 0, of which waited for: 2 -> 0; matrix products, arithmetic and copies ran while one was open for 0% -> 0% of each run, Pallas kernels for 0% -> 0%
where the time goes in v1:
time: 83.2 us; the launch traced here: 82.9 us
  Pallas kernels  71.5 us (86%)
  local copies, waits for them, and re-layouts  7.16 us (9%)
  between operations  2.43 us (3%)
  matrix products  1.76 us (2%)
    pallas_call x1, Pallas kernels, body(): pl.pallas_call(functools.partial(kernel, pn), out_shape=(jax.ShapeDtypeSt...  71.5 us
    unnamed x11, local copies, waits for them, and re-layouts  5.37 us
    dot_general x1, matrix products, body(): lax.dot_general(gp, weight, (((0,), (0,)), ((), ())), preferred_element_t...  1.76 us

profile of v1, /device:TPU:1, one launch (start us, length us, event | category | flops | bytes accessed | tf_op | source)
XLA Modules:
  0.0 82.9 jit_solution(4436099071142931415)
XLA Ops:
  0.6 0.7 broadcast_in_dim.13.area_hbm
  1.3 0.0 copy-start
  1.3 0.9 %copy-done = bf16[100,1024]{1,0:T(8,128)(2,1)S(1)} copy-done((bf16[100,1024]{1,0:T(8,128)(2,1)S(1)}, bf16[100,1024]{1,0:T(8,128)(2,1)}, u32[]{:S(2)}) %copy-start) | copy-done | bytes 204824
  2.3 0.0 copy-start.1
  2.3 1.4 %copy-done.1 = bf16[1,768,1024]{2,1,0:T(8,128)(2,1)S(1)} copy-done((bf16[1,768,1024]{2,1,0:T(8,128)(2,1)S(1)}, bf16[1,768,1024]{2,1,0:T(8,128)(2,1)}, u32[]{:S(2)}) %copy-start.1) | copy-done | bytes 1572888
  3.7 0.0 copy-start.2
  3.7 1.0 %copy-done.2 = f32[100,768]{1,0:T(8,128)S(1)} copy-done((f32[100,768]{1,0:T(8,128)S(1)}, f32[100,768]{1,0:T(8,128)}, u32[]{:S(2)}) %copy-start.2) | copy-done | bytes 307224
  4.6 0.0 copy-start.3
  4.6 0.7 copy-done.3
  5.3 0.0 copy-start.4
  5.3 0.7 copy-done.4
  5.9 71.5 %shard_map.93 = (bf16[100,768]{1,0:T(8,128)(2,1)S(1)}, f32[100,1024]{1,0:T(8,128)S(1)}, f32[1,128]{1,0:T(1,128)S(1)}) custom-call(bf16[768,1024]{1,0:T(8,128)(2,1)S(1)} %bitcast.10, bf16[100,1024]{1,0:T(8,128)(2,1)S(1)} %copy-done, f32[1,100]{1,0:T(1,128)S(1)} %bitcast.11, f32[100,768]{1,0:T(8,128)S(1)} %copy-done.2, ...), custom_call_target="tpu_custom_call" | custom-call | flops 314572800 | bytes 1572864 | tf_op jit(solution)/shard_map/pallas_call | solution.py:413
  77.5 0.6 slice.6
  78.7 0.5 slice_bitcast_fusion
  79.2 1.8 %fusion = bf16[1,768,1024]{2,1,0:T(8,128)(2,1)} fusion(bf16[100,768]{1,0:T(8,128)(2,1)S(1)} %get-tuple-element.8, bf16[100,1024]{1,0:T(8,128)(2,1)S(1)} %copy-done), kind=kOutput, calls=%fused_computation.1 | convolution fusion | flops 158072832 | bytes 1931264 | tf_op jit(solution)/shard_map/dot_general | solution.py:463
  81.0 0.8 copy.11
Async XLA Ops:
  1.3 0.9 %copy-start = (bf16[100,1024]{1,0:T(8,128)(2,1)S(1)}, bf16[100,1024]{1,0:T(8,128)(2,1)}, u32[]{:S(2)}) copy-start(bf16[100,1024]{1,0:T(8,128)(2,1)} %w_hbm.1) | copy-start | bytes 614404
  2.3 1.4 %copy-start.1 = (bf16[1,768,1024]{2,1,0:T(8,128)(2,1)S(1)}, bf16[1,768,1024]{2,1,0:T(8,128)(2,1)}, u32[]{:S(2)}) copy-start(bf16[1,768,1024]{2,1,0:T(8,128)(2,1)} %param.6) | copy-start | bytes 4718596
  3.7 1.0 %copy-start.2 = (f32[100,768]{1,0:T(8,128)S(1)}, f32[100,768]{1,0:T(8,128)}, u32[]{:S(2)}) copy-start(f32[100,768]{1,0:T(8,128)} %tgt_hbm.1) | copy-start | bytes 921604
  4.6 0.7 copy-start.3
  5.3 0.7 copy-start.4

commit v2 on v1

v2 whole, which is shorter than its diff:
```python
import functools

import jax
import jax.numpy as jnp
from jax import lax
from jax.experimental import pallas as pl
from jax.experimental.pallas import tpu as pltpu
from jax.sharding import PartitionSpec as P

alpha_fair = 0.95
smooth = 0.3
MESH = pl.DeviceIdType.MESH
F32 = jnp.float32
BF16 = jnp.bfloat16
XL = 2


class Plan:
    def __init__(self, mesh_shape, V, H, G):
        self.E, self.NG = mesh_shape["ens"], mesh_shape["grid"]
        self.V, self.H, self.G = V, H, G
        self.NZ = self.E // XL
        self.VG, self.REM = V // 16, V % 16
        self.NT, self.HC = G // 128, H // 128
        self.FOLD = 16 // self.REM
        self.RT = -(-self.NT // self.FOLD)
        self.FULL = self.VG * self.NT
        self.T = self.FULL + self.RT
        self.TAIL = self.T - self.E
        self.STEP = max(1, self.NZ // max(1, self.TAIL))
        self.PL = XL * self.NG
        mid = self.VG // 2
        self.WAVES = ((0, mid), (mid, self.VG))
        self.RW = -(-(self.REM * self.HC) // 16)
        self.GWT = tuple((b - a) * self.HC + (self.RW if b == self.VG else 0) for a, b in self.WAVES)
        self.GW0 = tuple(sum(self.GWT[:i]) for i in range(len(self.GWT)))
        self.OFF = (0, self.PL - self.GWT[-1])

    def tiles(self, wave):
        a, b = self.WAVES[wave]
        return a * self.NT, self.T if b == self.VG else b * self.NT

    def far_first(self, me, i):
        half = self.NZ // 2
        return (me + half + jnp.where(i % 2 == 1, (i + 1) // 2, self.NZ - i // 2)) % self.NZ

    def rank_of(self, e):
        z, xl = e // XL, e % XL
        return jnp.where(xl == z % 2, z, self.NZ + z)

    def owner(self, r):
        z = r % self.NZ
        return z * XL + (r + r // self.NZ) % 2


def kernel(pn, hid_hbm, w_hbm, bias_hbm, tgt_hbm, area_hbm, var_hbm, gp_ref, f_ref, x_ref,
           hid, w, bias, target, area, var, tgt, scl, varb, bcol, tmp, rem, S, R, G, B, pv, acc,
           xs, X, zx, PP, Q, zs, zr, U, F,
           in_sem, s_send, s_recv, g_send, b_recv, p_send, q_recv, z_send, z_recv, u_send, f_recv,
           x_send, x_recv, zx_send, zx_recv):
    E, NG, NZ, VG, REM, NT, HC = pn.E, pn.NG, pn.NZ, pn.VG, pn.REM, pn.NT, pn.HC
    V, FULL, T, TAIL, NPL = pn.V, pn.FULL, pn.T, pn.TAIL, pn.PL
    NW = len(pn.WAVES)
    e = lax.axis_index("ens")
    g = lax.axis_index("grid")
    myz, myx = e // XL, e % XL
    r = pn.rank_of(e)
    q = g * XL + myx

    def plane(k):
        return {"ens": myz * XL + k % XL, "grid": k // XL}

    def column(k):
        return {"ens": k * XL + myx}

    def landed(ref, sem):
        pltpu.make_async_copy(ref, ref, sem).wait()

    def send(src, dst, send_sem, recv_sem, where):
        pltpu.make_async_remote_copy(
            src_ref=src, dst_ref=dst, send_sem=send_sem, recv_sem=recv_sem, device_id=where, device_id_type=MESH).start()

    barrier = pltpu.get_barrier_semaphore()

    @pl.loop(0, NZ)
    def _(i):
        z = pn.far_first(myz, i)
        for xl in range(XL):
            @pl.when(z * XL + xl != e)
            def _():
                pl.semaphore_signal(barrier, inc=1, device_id={"ens": z * XL + xl}, device_id_type=MESH)

    ins = [(w_hbm, w), (bias_hbm, bias), (tgt_hbm, target), (area_hbm, area), (var_hbm, var)]
    in_copies = [pltpu.make_async_copy(a, b, in_sem.at[i]) for i, (a, b) in enumerate(ins)]
    hid_copies = [
        pltpu.make_async_copy(hid_hbm.at[pl.ds(t * 128, 128)], hid.at[pl.ds(t * 128, 128)], in_sem.at[len(ins) + t])
        for t in range(NT)
    ]
    in_copies[0].start()
    in_copies[1].start()
    for c in hid_copies:
        c.start()
    for c in in_copies[2:]:
        c.start()

    @pl.loop(1, NPL)
    def _(i):
        pl.semaphore_signal(barrier, inc=1, device_id=plane(lax.rem(q + i, NPL)), device_id_type=MESH)

    in_copies[0].wait()
    in_copies[1].wait()
    varb[...] = jnp.zeros_like(varb)
    varb[:, 0:V] = jnp.broadcast_to(bias[...], (128, V))
    biasb = varb[...].T[0:V]
    rem[...] = jnp.zeros_like(rem)
    for t in range(NT):
        hid_copies[t].wait()
        raw = lax.dot_general(w[...], hid[t * 128:(t + 1) * 128], (((1,), (1,)), ((), ())), preferred_element_type=F32)
        pred = raw + biasb
        for vg in range(VG):
            S[vg * NT + t] = pred[16 * vg:16 * vg + 16].astype(BF16)
        rem[REM * t:REM * t + REM] = pred[16 * VG:V]
    for i in range(pn.RT):
        S[FULL + i] = rem[16 * i:16 * i + 16].astype(BF16)

    pl.semaphore_wait(barrier, E - 1 + NPL - 1)

    def send_tile(slot, j, rank):
        own = pn.owner(rank)

        @pl.when(own == e)
        def _():
            pltpu.make_async_copy(S.at[j], R.at[slot, e], s_recv.at[slot]).start()

        @pl.when(own != e)
        def _():
            send(S.at[j], R.at[slot, e], s_send.at[slot], s_recv.at[slot], {"ens": own})

    for wave in range(NW):
        lo, hi = pn.tiles(wave)

        @pl.loop(0, NZ)
        def _(i):
            z = pn.far_first(myz, i)
            for part in range(XL):
                if max(lo, part * NZ) < min(hi, part * NZ + NZ):
                    rank = z + part * NZ

                    @pl.when(jnp.logical_and(rank >= lo, rank < hi))
                    def _():
                        send_tile(0, rank, rank)

    @pl.loop(0, TAIL)
    def _(i):
        send_tile(1, E + i, i * pn.STEP)

    for c in in_copies[2:]:
        c.wait()
    varb[:, 0:V] = jnp.broadcast_to(var[...], (128, V))
    varb[...] = varb[...].T
    bcol[...] = jnp.zeros_like(bcol)

    tail_i = r // pn.STEP
    has_tail = jnp.logical_and(r % pn.STEP == 0, tail_i < TAIL)

    def prepare(slot, j):
        @pl.when(j < FULL)
        def _():
            vrow = pl.multiple_of((j // NT) * 16, 16)
            col = pl.multiple_of((j % NT) * 128, 128)
            tgt[slot] = target[pl.ds(vrow, 16), pl.ds(col, 128)]
            scl[slot] = varb[pl.ds(vrow, 16)] * area[pl.ds(j % NT, 1)]

        for i in range(pn.RT):
            @pl.when(j == FULL + i)
            def _():
                tgt[slot] = jnp.zeros((16, 128), F32)
                scl[slot] = jnp.zeros((16, 128), F32)
                for k in range(pn.FOLD):
                    t = i * pn.FOLD + k
                    if t < NT:
                        cols = slice(128 * t, 128 * t + 128)
                        tgt[slot, REM * k:REM * k + REM] = target[16 * VG:V, cols]
                        scl[slot, REM * k:REM * k + REM] = varb[16 * VG:V] * area[t:t + 1]

    prepare(0, r)

    @pl.when(has_tail)
    def _():
        prepare(1, E + tail_i)

    members = E
    eps = (1.0 - alpha_fair) / members
    pair_coef = (1.0 - eps) / (members - 1)
    c2 = smooth * smooth
    BM = min(8, E // 2)
    NB = E // BM

    def blocks(h, i, j, total, diag):
        rows = pl.ds(h * 8, 8)
        a = [pv[i * BM + k, rows] for k in range(BM)]
        b = a if diag else [pv[j * BM + k, rows] for k in range(BM)]
        sa = [acc[i * BM + k, rows] for k in range(BM)]
        sb = sa if diag else [acc[j * BM + k, rows] for k in range(BM)]
        for m in range(BM):
            for k in range(m + 1 if diag else 0, BM):
                d = a[m] - b[k]
                qq = d * d + c2
                rs = lax.rsqrt(qq)
                s = d * rs
                total = total + qq * rs
                sa[m] = sa[m] + s
                sb[k] = sb[k] - s
        for k in range(BM):
            acc[i * BM + k, rows] = sa[k]
            if not diag:
                acc[j * BM + k, rows] = sb[k]
        return total

    def process(slot, j):
        landed(R.at[slot], s_recv.at[slot])
        for m in range(E):
            pv[m] = R[slot, m].astype(F32)
            acc[m] = jnp.zeros((16, 128), F32)

        def half(h, _):
            total = lax.fori_loop(0, NB, lambda i, t: blocks(h, i, i, t, True), jnp.zeros((8, 128), F32))

            def off(k, t):
                if NB == 2:
                    return blocks(h, 0, 1, t, False)
                return blocks(h, k % 4, (k + 1 + k // 4) % 4, t, False)
            tmp[pl.ds(h * 8, 8)] = lax.fori_loop(0, NB * (NB - 1) // 2, off, total)
            return 0
        lax.fori_loop(0, 2, half, 0)
        tg, sc = tgt[slot], scl[slot]
        wave = jnp.where(j >= pn.tiles(NW - 1)[0], NW - 1, 0)

        def finish(i, carry):
            bsum, absum = carry
            z = pn.far_first(myz, i)
            for xl in range(XL):
                m = z * XL + xl
                d = pv[m] - tg
                qq = d * d + c2
                rs = lax.rsqrt(qq)
                gb = (sc * (d * rs - pair_coef * acc[m])).astype(BF16)
                G[slot, m] = gb
                bsum, absum = bsum + gb.astype(F32), absum + qq * rs

                @pl.when(m == e)
                def _():
                    pltpu.make_async_copy(G.at[slot, m], B.at[j], b_recv.at[wave]).start()

                @pl.when(m != e)
                def _():
                    send(G.at[slot, m], B.at[j], g_send.at[slot], b_recv.at[wave], {"ens": m})
            return bsum, absum
        zero = jnp.zeros((16, 128), F32)
        bsum, absum = lax.fori_loop(0, NZ, finish, (zero, zero))

        npair = members * (members - 1) // 2
        crps = (absum - members * smooth) / members - 2.0 * (pair_coef / (2.0 * members)) * (tmp[...] - npair * smooth)
        lossb = jnp.broadcast_to(jnp.sum(sc * crps, axis=(0, 1), keepdims=True), (8, 128))
        bcol[V + 4:V + 12] = bcol[V + 4:V + 12] + lossb
        bb = jnp.broadcast_to(jnp.sum(bsum, axis=1, keepdims=True), (16, 128))

        @pl.when(j < FULL)
        def _():
            rows = pl.ds(pl.multiple_of((j // NT) * 16, 16), 16)
            bcol[rows] = bcol[rows] + bb

        @pl.when(j >= FULL)
        def _():
            tmp[...] = bb
            fold = tmp[0:REM]
            for k in range(1, pn.FOLD):
                fold = fold + tmp[REM * k:REM * k + REM]
            bcol[16 * VG:V] = bcol[16 * VG:V] + fold

    process(0, r)

    @pl.when(has_tail)
    def _():
        process(1, E + tail_i)

    xs[...] = bcol[...].T[0:1]
    X[q] = xs[...]

    @pl.loop(1, NPL)
    def _(i):
        send(xs, X.at[q], x_send, x_recv, plane(lax.rem(q + i, NPL)))

    def home(wave):
        lo, hi = pn.tiles(wave)
        a, b = pn.WAVES[wave]
        last = b == VG
        landed(B.at[pl.ds(lo, hi - lo)], b_recv.at[wave])
        for t in range(NT):
            for vg in range(a, b):
                gp_ref[16 * vg:16 * vg + 16, 128 * t:128 * t + 128] = B[vg * NT + t]
        if last:
            for i in range(pn.RT):
                rem[16 * i:16 * i + 16] = B[FULL + i].astype(F32)
            for t in range(NT):
                gp_ref[16 * VG:V, 128 * t:128 * t + 128] = rem[REM * t:REM * t + REM].astype(BF16)
        rows = slice(16 * a, V if last else 16 * b)
        CW = 256
        n0 = pn.GW0[wave]
        for cc in range(pn.H // CW):
            part = lax.dot_general(
                gp_ref[rows], hid[:, cc * CW:(cc + 1) * CW], (((1,), (0,)), ((), ())), preferred_element_type=F32)
            for c2_ in range(CW // 128):
                c = cc * (CW // 128) + c2_
                cols = slice(128 * c2_, 128 * c2_ + 128)
                for vg in range(b - a):
                    PP[n0 + c * (b - a) + vg] = part[16 * vg:16 * vg + 16, cols].astype(BF16)
                if last:
                    rem[REM * c:REM * c + REM] = part[16 * (b - a):, cols]
        if last:
            for i in range(pn.RW):
                PP[n0 + HC * (b - a) + i] = rem[16 * i:16 * i + 16].astype(BF16)

        @pl.loop(0, NPL)
        def _(i):
            k = lax.rem(q + i, NPL)
            n = lax.rem(k + NPL - pn.OFF[wave], NPL)

            @pl.when(jnp.logical_and(n < pn.GWT[wave], k == q))
            def _():
                pltpu.make_async_copy(PP.at[n0 + n], Q.at[wave, q], q_recv.at[wave]).start()

            @pl.when(jnp.logical_and(n < pn.GWT[wave], k != q))
            def _():
                send(PP.at[n0 + n], Q.at[wave, q], p_send.at[wave], q_recv.at[wave], plane(k))

    for wave in range(NW):
        home(wave)

    landed(X.at[pl.ds(0, NPL - 1)], x_recv)
    zx[myz] = lax.fori_loop(1, NPL, lambda i, s: s + X[i], X[0])

    @pl.loop(0, NZ - 1)
    def _(i):
        send(zx.at[myz], zx.at[myz], zx_send, zx_recv, column(pn.far_first(myz, i)))

    points = pn.G * NG
    mine = [lax.rem(q + NPL - pn.OFF[wave], NPL) for wave in range(NW)]

    for wave in range(NW):
        @pl.when(mine[wave] < pn.GWT[wave])
        def _():
            landed(Q.at[wave], q_recv.at[wave])
            total = Q[wave, 0].astype(F32)
            for i in range(1, NPL):
                total = total + Q[wave, i].astype(F32)
            zs[wave] = total.astype(BF16)
            zr[wave, myz] = total.astype(BF16)

            @pl.loop(0, NZ - 1)
            def _(i):
                send(zs.at[wave], zr.at[wave, myz], z_send.at[wave], z_recv.at[wave], column(pn.far_first(myz, i)))

    for wave in range(NW):
        @pl.when(mine[wave] < pn.GWT[wave])
        def _():
            landed(zr.at[wave, pl.ds(0, NZ - 1)], z_recv.at[wave])
            total = zr[wave, 0].astype(F32)
            for i in range(1, NZ):
                total = total + zr[wave, i].astype(F32)
            U[wave] = (total * (1.0 / points)).astype(BF16)
            dst = F.at[pn.GW0[wave] + mine[wave]]
            pltpu.make_async_copy(U.at[wave], dst, f_recv.at[wave]).start()

            @pl.loop(1, NPL)
            def _(i):
                send(U.at[wave], dst, u_send.at[wave], f_recv.at[wave], plane(lax.rem(q + i, NPL)))

    landed(zx.at[pl.ds(0, NZ - 1)], zx_recv)
    x_ref[...] = lax.fori_loop(0, NZ, lambda i, s: s + zx[i], jnp.zeros((1, 128), F32)) * (1.0 / points)

    landed(S.at[pl.ds(0, E - 1)], s_send.at[0])
    landed(G.at[0, pl.ds(0, E - 1)], g_send.at[0])
    landed(X.at[pl.ds(0, NPL - 1)], x_send)
    landed(zx.at[pl.ds(0, NZ - 1)], zx_send)

    @pl.when(has_tail)
    def _():
        landed(S.at[pl.ds(0, TAIL - 1)], s_send.at[1])
        landed(G.at[1, pl.ds(0, E - 1)], g_send.at[1])

    @pl.when(jnp.logical_not(has_tail))
    def _():
        landed(S.at[pl.ds(0, TAIL)], s_send.at[1])

    for wave in range(NW):
        n = pn.GWT[wave]

        @pl.when(mine[wave] < n)
        def _():
            landed(PP.at[pl.ds(0, n - 1)], p_send.at[wave])
            landed(zr.at[wave, pl.ds(0, NZ - 1)], z_send.at[wave])
            landed(Q.at[wave, pl.ds(0, NPL - 1)], u_send.at[wave])

        @pl.when(mine[wave] >= n)
        def _():
            landed(PP.at[pl.ds(0, n)], p_send.at[wave])

    for wave in range(NW):
        n0, n = pn.GW0[wave], pn.GWT[wave]
        landed(F.at[pl.ds(n0, n)], f_recv.at[wave])
        f_ref[n0:n0 + n] = F[n0:n0 + n]


def finish_kernel(pn, gp, w, f, x, loss_ref, gh_hbm, gw_hbm, gb_ref, gw, gh, rem, sems):
    V, VG, REM, HC = pn.V, pn.VG, pn.REM, pn.HC
    for wave, (a, b) in enumerate(pn.WAVES):
        for c in range(HC):
            for vg in range(a, b):
                gw[16 * vg:16 * vg + 16, 128 * c:128 * c + 128] = f[pn.GW0[wave] + c * (b - a) + vg - a].astype(F32)
    for i in range(pn.RW):
        rem[16 * i:16 * i + 16] = f[pn.GW0[-1] + pn.GWT[-1] - pn.RW + i].astype(F32)
    for c in range(HC):
        gw[16 * VG:V, 128 * c:128 * c + 128] = rem[REM * c:REM * c + REM]
    copies = [pltpu.make_async_copy(gw, gw_hbm, sems.at[0])]
    copies[0].start()
    for t in range(pn.NT):
        rows = slice(128 * t, 128 * t + 128)
        gh[rows] = lax.dot_general(
            gp[:, rows], w[...], (((0,), (0,)), ((), ())), preferred_element_type=F32).astype(BF16)
        out = pltpu.make_async_copy(gh.at[pl.ds(128 * t, 128)], gh_hbm.at[pl.ds(128 * t, 128)], sems.at[1 + t])
        out.start()
        copies.append(out)
    gb_ref[...] = x[0:1, 0:V]
    loss_ref[...] = x[0:1, V + 4:V + 5] * (1.0 / V)
    for out in copies:
        out.wait()


def body(mesh_shape, hidden, weight, bias, target, area_weight, var_weight):
    rows = hidden[0]
    V, H = weight.shape
    G = rows.shape[0]
    pn = Plan(mesh_shape, V, H, G)
    E, NZ = pn.E, pn.NZ
    NW = len(pn.WAVES)
    tile = (16, 128)
    NF = sum(pn.GWT)
    dma = pltpu.SemaphoreType.DMA
    vmem = pl.BlockSpec(memory_space=pltpu.VMEM)
    anywhere = pl.BlockSpec(memory_space=pl.ANY)
    gp, f, x = pl.pallas_call(
        functools.partial(kernel, pn),
        out_shape=(
            jax.ShapeDtypeStruct((V, G), BF16),
            jax.ShapeDtypeStruct((NF,) + tile, BF16),
            jax.ShapeDtypeStruct((1, 128), F32),
        ),
        in_specs=[anywhere] * 6,
        out_specs=(vmem,) * 3,
        scratch_shapes=[
            pltpu.VMEM((G, H), BF16),
            pltpu.VMEM((V, H), BF16),
            pltpu.VMEM((1, V), F32),
            pltpu.VMEM((V, G), F32),
            pltpu.VMEM((pn.NT, 128), F32),
            pltpu.VMEM((1, V), F32),
            pltpu.VMEM((2,) + tile, F32),
            pltpu.VMEM((2,) + tile, F32),
            pltpu.VMEM((128, 128), F32),
            pltpu.VMEM((128, 128), F32),
            pltpu.VMEM(tile, F32),
            pltpu.VMEM((32, 128), F32),
            pltpu.VMEM((pn.T,) + tile, BF16),
            pltpu.VMEM((2, E) + tile, BF16),
            pltpu.VMEM((2, E) + tile, BF16),
            pltpu.VMEM((pn.T,) + tile, BF16),
            pltpu.VMEM((E,) + tile, F32),
            pltpu.VMEM((E,) + tile, F32),
            pltpu.VMEM((1, 128), F32),
            pltpu.VMEM((pn.PL, 1, 128), F32),
            pltpu.VMEM((NZ, 1, 128), F32),
            pltpu.VMEM((NF,) + tile, BF16),
            pltpu.VMEM((NW, pn.PL) + tile, BF16),
            pltpu.VMEM((NW,) + tile, BF16),
            pltpu.VMEM((NW, NZ) + tile, BF16),
            pltpu.VMEM((NW,) + tile, BF16),
            pltpu.VMEM((NF,) + tile, BF16),
            dma((5 + pn.NT,)),
            dma((2,)),
            dma((2,)),
            dma((2,)),
            dma((NW,)),
            dma((NW,)),
            dma((NW,)),
            dma((NW,)),
            dma((NW,)),
            dma((NW,)),
            dma((NW,)),
            dma, dma, dma, dma,
        ],
        compiler_params=pltpu.CompilerParams(
            collective_id=0, has_side_effects=True, vmem_limit_bytes=60 * 1024 * 1024
        ),
        cost_estimate=pl.CostEstimate(flops=4 * V * G * H, bytes_accessed=2 * G * H, transcendentals=V * G * 16),
    )(rows, weight, bias[None], target, area_weight.reshape(-1, 128), var_weight[None])
    loss, gh, gw, gb = pl.pallas_call(
        functools.partial(finish_kernel, pn),
        out_shape=(
            jax.ShapeDtypeStruct((1, 1), F32),
            jax.ShapeDtypeStruct((G, H), BF16),
            jax.ShapeDtypeStruct((V, H), F32),
            jax.ShapeDtypeStruct((1, V), F32),
        ),
        in_specs=[vmem] * 4,
        out_specs=(vmem, anywhere, anywhere, vmem),
        scratch_shapes=[
            pltpu.VMEM((V, H), F32),
            pltpu.VMEM((G, H), BF16),
            pltpu.VMEM((32, 128), F32),
            dma((1 + pn.NT,)),
        ],
        compiler_params=pltpu.CompilerParams(vmem_limit_bytes=60 * 1024 * 1024),
        cost_estimate=pl.CostEstimate(flops=2 * V * G * H, bytes_accessed=2 * G * H, transcendentals=0),
    )(gp, weight, f, x)
    return (loss[0, 0], gh[None], gw, gb[0])


def solution(mesh):
    return jax.shard_map(
        functools.partial(body, dict(mesh.shape)),
        mesh=mesh,
        in_specs=(P("ens", "grid", None), P(), P(), P(None, "grid"), P("grid"), P()),
        out_specs=(P(), P("ens", "grid", None), P(), P()),
        check_vma=False,
    )
```

time: 83.2 us -> 62.6 us (0.75)
  Pallas kernels: 71.5 us -> 61.8 us
  local copies, waits for them, and re-layouts: 7.16 us -> 0 us
  between operations: 2.43 us -> 0.64 us
  matrix products: 1.76 us -> 0 us
    pallas_call x1, Pallas kernels: 71.5 us -> 58.6 us  [body(): pl.pallas_call(functools.partial(kernel, pn), out_shape=(jax.ShapeDtypeSt...]
    unnamed x11 -> x0, local copies, waits for them, and re-layouts: 5.37 us -> none
    pallas_call x0 -> x1, Pallas kernels: none -> 3.17 us  [body(): pl.pallas_call(functools.partial(finish_kernel, pn), out_shape=(jax.Shape...]
    dot_general x1 -> x0, matrix products: 1.76 us -> none  [body(): lax.dot_general(gp, weight, (((0,), (0,)), ((), ())), preferred_element_t...]
where the time goes in v2:
time: 62.6 us; the launch traced here: 62.4 us
  Pallas kernels  61.8 us (99%)
  between operations  0.64 us (1%)
    pallas_call x1, Pallas kernels, body(): pl.pallas_call(functools.partial(kernel, pn), out_shape=(jax.ShapeDtypeSt...  58.6 us
    pallas_call x1, Pallas kernels, body(): pl.pallas_call(functools.partial(finish_kernel, pn), out_shape=(jax.Shape...  3.17 us

profile of v2, /device:TPU:1, one launch (start us, length us, event | category | flops | bytes accessed | tf_op | source)
XLA Modules:
  0.0 62.4 jit_solution(13564389168236106543)
XLA Ops:
  0.6 58.6 %shard_map.93 = (bf16[100,768]{1,0:T(8,128)(2,1)}, bf16[50,16,128]{2,1,0:T(8,128)(2,1)}, f32[1,128]{1,0:T(1,128)}) custom-call(bf16[768,1024]{1,0:T(8,128)(2,1)} %bitcast.7, bf16[100,1024]{1,0:T(8,128)(2,1)} %w.1, f32[1,100]{1,0:T(1,128)} %bitcast.9, f32[100,768]{1,0:T(8,128)} %tgt_hbm.1, f32[6,128]{1,0:T(8,128)} %bitcast.8, f32[1,100]{1,0:T(1,128)} %bitcast.10), custom_call_target="tpu_custom_call" | custom-call | flops 314572800 | bytes 1572864 | tf_op jit(solution)/shard_map/pallas_call | solution.py:452
  59.3 3.2 %shard_map.94 = (f32[1,1]{1,0:T(1,128)}, bf16[768,1024]{1,0:T(8,128)(2,1)}, f32[100,1024]{1,0:T(8,128)}, f32[1,100]{1,0:T(1,128)}) custom-call(bf16[100,768]{1,0:T(8,128)(2,1)} %get-tuple-element.11.gp, bf16[100,1024]{1,0:T(8,128)(2,1)} %w.1, bf16[50,16,128]{2,1,0:T(8,128)(2,1)} %get-tuple-element.12.f, f32[1,128]{1,0:T(1,128)} %get-tuple-element.13.x), custom_call_target="tpu_custom_call" | custom-call | flops 157286400 | bytes 1572864 | tf_op jit(solution)/shard_map/pallas_call | solution.py:507

commit v3 on v2

--- a/solution.py
+++ b/solution.py
@@ -29,17 +29,29 @@
         self.TAIL = self.T - self.E
         self.STEP = max(1, self.NZ // max(1, self.TAIL))
         self.PL = XL * self.NG
-        mid = self.VG // 2
-        self.WAVES = ((0, mid), (mid, self.VG))
+        nw = min(2, self.VG)
+        cuts = [self.VG * i // nw for i in range(nw + 1)]
+        self.WAVES = tuple(zip(cuts[:-1], cuts[1:]))
         self.RW = -(-(self.REM * self.HC) // 16)
         self.GWT = tuple((b - a) * self.HC + (self.RW if b == self.VG else 0) for a, b in self.WAVES)
         self.GW0 = tuple(sum(self.GWT[:i]) for i in range(len(self.GWT)))
-        self.OFF = (0, self.PL - self.GWT[-1])
 
     def tiles(self, wave):
         a, b = self.WAVES[wave]
         return a * self.NT, self.T if b == self.VG else b * self.NT
 
+    def wave_of(self, j):
+        wave = 0
+        for k in range(1, len(self.WAVES)):
+            wave = wave + jnp.where(j >= self.tiles(k)[0], 1, 0)
+        return wave
+
+    def owned(self, q, wave):
+        return q // 4 * 2 + q % 2 + self.PL // 2 * ((q // 2 + wave) % 2)
+
+    def plane_peer(self, q, i):
+        return lax.rem(q + 1 + i, self.PL)
+
     def far_first(self, me, i):
         half = self.NZ // 2
         return (me + half + jnp.where(i % 2 == 1, (i + 1) // 2, self.NZ - i // 2)) % self.NZ
@@ -53,11 +65,11 @@
         return z * XL + (r + r // self.NZ) % 2
 
 
-def kernel(pn, hid_hbm, w_hbm, bias_hbm, tgt_hbm, area_hbm, var_hbm, gp_ref, f_ref, x_ref,
-           hid, w, bias, target, area, var, tgt, scl, varb, bcol, tmp, rem, S, R, G, B, pv, acc,
+def kernel(pn, hid_hbm, w_hbm, bias_hbm, tgt_hbm, area_hbm, var_hbm, gp_hbm, f_hbm, x_ref,
+           gp_ref, hid, w, bias, target, area, var, tgt, scl, varb, bcol, tmp, rem, S, R, G, B, pv, acc,
            xs, X, zx, PP, Q, zs, zr, U, F,
            in_sem, s_send, s_recv, g_send, b_recv, p_send, q_recv, z_send, z_recv, u_send, f_recv,
-           x_send, x_recv, zx_send, zx_recv):
+           out_sem, x_send, x_recv, zx_send, zx_recv):
     E, NG, NZ, VG, REM, NT, HC = pn.E, pn.NG, pn.NZ, pn.VG, pn.REM, pn.NT, pn.HC
     V, FULL, T, TAIL, NPL = pn.V, pn.FULL, pn.T, pn.TAIL, pn.PL
     NW = len(pn.WAVES)
@@ -103,9 +115,9 @@
     for c in in_copies[2:]:
         c.start()
 
-    @pl.loop(1, NPL)
+    @pl.loop(0, NPL - 1)
     def _(i):
-        pl.semaphore_signal(barrier, inc=1, device_id=plane(lax.rem(q + i, NPL)), device_id_type=MESH)
+        pl.semaphore_signal(barrier, inc=1, device_id=plane(pn.plane_peer(q, i)), device_id_type=MESH)
 
     in_copies[0].wait()
     in_copies[1].wait()
@@ -193,8 +205,7 @@
     eps = (1.0 - alpha_fair) / members
     pair_coef = (1.0 - eps) / (members - 1)
     c2 = smooth * smooth
-    BM = min(8, E // 2)
-    NB = E // BM
+    BM = E // 2
 
     def blocks(h, i, j, total, diag):
         rows = pl.ds(h * 8, 8)
@@ -223,18 +234,13 @@
             pv[m] = R[slot, m].astype(F32)
             acc[m] = jnp.zeros((16, 128), F32)
 
-        def half(h, _):
-            total = lax.fori_loop(0, NB, lambda i, t: blocks(h, i, i, t, True), jnp.zeros((8, 128), F32))
-
-            def off(k, t):
-                if NB == 2:
-                    return blocks(h, 0, 1, t, False)
-                return blocks(h, k % 4, (k + 1 + k // 4) % 4, t, False)
-            tmp[pl.ds(h * 8, 8)] = lax.fori_loop(0, NB * (NB - 1) // 2, off, total)
-            return 0
-        lax.fori_loop(0, 2, half, 0)
+        @pl.loop(0, 2)
+        def _(h):
+            total = blocks(h, 0, 0, jnp.zeros((8, 128), F32), True)
+            total = blocks(h, 1, 1, total, True)
+            tmp[pl.ds(h * 8, 8)] = blocks(h, 0, 1, total, False)
         tg, sc = tgt[slot], scl[slot]
-        wave = jnp.where(j >= pn.tiles(NW - 1)[0], NW - 1, 0)
+        wave = pn.wave_of(j)
 
         def finish(i, carry):
             bsum, absum = carry
@@ -278,18 +284,18 @@
                 fold = fold + tmp[REM * k:REM * k + REM]
             bcol[16 * VG:V] = bcol[16 * VG:V] + fold
 
-    process(0, r)
-
-    @pl.when(has_tail)
-    def _():
-        process(1, E + tail_i)
+    @pl.loop(0, 2)
+    def _(slot):
+        @pl.when(jnp.logical_or(slot == 0, has_tail))
+        def _():
+            process(slot, jnp.where(slot == 0, r, E + tail_i))
 
     xs[...] = bcol[...].T[0:1]
     X[q] = xs[...]
 
-    @pl.loop(1, NPL)
+    @pl.loop(0, NPL - 1)
     def _(i):
-        send(xs, X.at[q], x_send, x_recv, plane(lax.rem(q + i, NPL)))
+        send(xs, X.at[q], x_send, x_recv, plane(pn.plane_peer(q, i)))
 
     def home(wave):
         lo, hi = pn.tiles(wave)
@@ -323,8 +329,8 @@
 
         @pl.loop(0, NPL)
         def _(i):
-            k = lax.rem(q + i, NPL)
-            n = lax.rem(k + NPL - pn.OFF[wave], NPL)
+            k = pn.plane_peer(q, i)
+            n = pn.owned(k, wave)
 
             @pl.when(jnp.logical_and(n < pn.GWT[wave], k == q))
             def _():
@@ -336,6 +342,8 @@
 
     for wave in range(NW):
         home(wave)
+    out_copies = [pltpu.make_async_copy(gp_ref, gp_hbm, out_sem.at[0])]
+    out_copies[0].start()
 
     landed(X.at[pl.ds(0, NPL - 1)], x_recv)
     zx[myz] = lax.fori_loop(1, NPL, lambda i, s: s + X[i], X[0])
@@ -345,7 +353,7 @@
         send(zx.at[myz], zx.at[myz], zx_send, zx_recv, column(pn.far_first(myz, i)))
 
     points = pn.G * NG
-    mine = [lax.rem(q + NPL - pn.OFF[wave], NPL) for wave in range(NW)]
+    mine = [pn.owned(q, wave) for wave in range(NW)]
 
     for wave in range(NW):
         @pl.when(mine[wave] < pn.GWT[wave])
@@ -372,9 +380,9 @@
             dst = F.at[pn.GW0[wave] + mine[wave]]
             pltpu.make_async_copy(U.at[wave], dst, f_recv.at[wave]).start()
 
-            @pl.loop(1, NPL)
+            @pl.loop(0, NPL - 1)
             def _(i):
-                send(U.at[wave], dst, u_send.at[wave], f_recv.at[wave], plane(lax.rem(q + i, NPL)))
+                send(U.at[wave], dst, u_send.at[wave], f_recv.at[wave], plane(pn.plane_peer(q, i)))
 
     landed(zx.at[pl.ds(0, NZ - 1)], zx_recv)
     x_ref[...] = lax.fori_loop(0, NZ, lambda i, s: s + zx[i], jnp.zeros((1, 128), F32)) * (1.0 / points)
@@ -409,7 +417,10 @@
     for wave in range(NW):
         n0, n = pn.GW0[wave], pn.GWT[wave]
         landed(F.at[pl.ds(n0, n)], f_recv.at[wave])
-        f_ref[n0:n0 + n] = F[n0:n0 + n]
+        out_copies.append(pltpu.make_async_copy(F.at[pl.ds(n0, n)], f_hbm.at[pl.ds(n0, n)], out_sem.at[1 + wave]))
+        out_copies[-1].start()
+    for c in out_copies:
+        c.wait()
 
 
 def finish_kernel(pn, gp, w, f, x, loss_ref, gh_hbm, gw_hbm, gb_ref, gw, gh, rem, sems):
@@ -457,8 +468,9 @@
             jax.ShapeDtypeStruct((1, 128), F32),
         ),
         in_specs=[anywhere] * 6,
-        out_specs=(vmem,) * 3,
+        out_specs=(anywhere, anywhere, vmem),
         scratch_shapes=[
+            pltpu.VMEM((V, G), BF16),
             pltpu.VMEM((G, H), BF16),
             pltpu.VMEM((V, H), BF16),
             pltpu.VMEM((1, V), F32),
@@ -497,6 +509,7 @@
             dma((NW,)),
             dma((NW,)),
             dma((NW,)),
+            dma((1 + NW,)),
             dma, dma, dma, dma,
         ],
         compiler_params=pltpu.CompilerParams(

time: 62.6 us -> 62.3 us (level)
  no operation moved by 1% of the time
where the time goes in v3:
time: 62.3 us; the launch traced here: 62.1 us
  Pallas kernels  61.5 us (99%)
  between operations  0.64 us (1%)
    pallas_call x1, Pallas kernels, body(): pl.pallas_call(functools.partial(kernel, pn), out_shape=(jax.ShapeDtypeSt...  58.3 us
    pallas_call x1, Pallas kernels, body(): pl.pallas_call(functools.partial(finish_kernel, pn), out_shape=(jax.Shape...  3.18 us

profile of v3, /device:TPU:1, one launch (start us, length us, event | category | flops | bytes accessed | tf_op | source)
XLA Modules:
  0.0 62.1 jit_solution(5690696181293525143)
XLA Ops:
  0.6 58.3 %shard_map.93 = (bf16[100,768]{1,0:T(8,128)(2,1)}, bf16[50,16,128]{2,1,0:T(8,128)(2,1)}, f32[1,128]{1,0:T(1,128)}) custom-call(bf16[768,1024]{1,0:T(8,128)(2,1)} %bitcast.7, bf16[100,1024]{1,0:T(8,128)(2,1)} %w.1, f32[1,100]{1,0:T(1,128)} %bitcast.9, f32[100,768]{1,0:T(8,128)} %tgt_hbm.1, f32[6,128]{1,0:T(8,128)} %bitcast.8, f32[1,100]{1,0:T(1,128)} %bitcast.10), custom_call_target="tpu_custom_call" | custom-call | flops 314572800 | bytes 1572864 | tf_op jit(solution)/shard_map/pallas_call | solution.py:463
  58.9 3.2 %shard_map.94 = (f32[1,1]{1,0:T(1,128)}, bf16[768,1024]{1,0:T(8,128)(2,1)}, f32[100,1024]{1,0:T(8,128)}, f32[1,100]{1,0:T(1,128)}) custom-call(bf16[100,768]{1,0:T(8,128)(2,1)} %get-tuple-element.11.gp, bf16[100,1024]{1,0:T(8,128)(2,1)} %w.1, bf16[50,16,128]{2,1,0:T(8,128)(2,1)} %get-tuple-element.12.f, f32[1,128]{1,0:T(1,128)} %get-tuple-element.13.x), custom_call_target="tpu_custom_call" | custom-call | flops 157286400 | bytes 1572864 | tf_op jit(solution)/shard_map/pallas_call | solution.py:520

commit v4 on v3

--- a/solution.py
+++ b/solution.py
@@ -47,7 +47,7 @@
         return wave
 
     def owned(self, q, wave):
-        return q // 4 * 2 + q % 2 + self.PL // 2 * ((q // 2 + wave) % 2)
+        return lax.div(q, 4) * 2 + lax.rem(q, 2) + self.PL // 2 * lax.rem(lax.div(q, 2) + wave, 2)
 
     def plane_peer(self, q, i):
         return lax.rem(q + 1 + i, self.PL)
@@ -80,7 +80,7 @@
     q = g * XL + myx
 
     def plane(k):
-        return {"ens": myz * XL + k % XL, "grid": k // XL}
+        return {"ens": myz * XL + lax.rem(k, XL), "grid": lax.div(k, XL)}
 
     def column(k):
         return {"ens": k * XL + myx}
@@ -329,7 +329,7 @@
 
         @pl.loop(0, NPL)
         def _(i):
-            k = pn.plane_peer(q, i)
+            k = lax.rem(q + NPL // 2 + i, NPL)
             n = pn.owned(k, wave)
 
             @pl.when(jnp.logical_and(n < pn.GWT[wave], k == q))
@@ -380,9 +380,13 @@
             dst = F.at[pn.GW0[wave] + mine[wave]]
             pltpu.make_async_copy(U.at[wave], dst, f_recv.at[wave]).start()
 
-            @pl.loop(0, NPL - 1)
+            @pl.loop(0, NPL)
             def _(i):
-                send(U.at[wave], dst, u_send.at[wave], f_recv.at[wave], plane(pn.plane_peer(q, i)))
+                k = lax.rem(q + NPL // 2 + i, NPL)
+
+                @pl.when(k != q)
+                def _():
+                    send(U.at[wave], dst, u_send.at[wave], f_recv.at[wave], plane(k))
 
     landed(zx.at[pl.ds(0, NZ - 1)], zx_recv)
     x_ref[...] = lax.fori_loop(0, NZ, lambda i, s: s + zx[i], jnp.zeros((1, 128), F32)) * (1.0 / points)

time: 62.3 us -> 61.7 us (level)
  no operation moved by 1% of the time
where the time goes in v4:
time: 61.7 us; the launch traced here: 61.6 us
  Pallas kernels  60.9 us (99%)
  between operations  0.64 us (1%)
    pallas_call x1, Pallas kernels, body(): pl.pallas_call(functools.partial(kernel, pn), out_shape=(jax.ShapeDtypeSt...  57.8 us
    pallas_call x1, Pallas kernels, body(): pl.pallas_call(functools.partial(finish_kernel, pn), out_shape=(jax.Shape...  3.18 us

profile of v4, /device:TPU:1, one launch (start us, length us, event | category | flops | bytes accessed | tf_op | source)
XLA Modules:
  0.0 61.6 jit_solution(16035994935499756851)
XLA Ops:
  0.6 57.8 %shard_map.93 = (bf16[100,768]{1,0:T(8,128)(2,1)}, bf16[50,16,128]{2,1,0:T(8,128)(2,1)}, f32[1,128]{1,0:T(1,128)}) custom-call(bf16[768,1024]{1,0:T(8,128)(2,1)} %bitcast.7, bf16[100,1024]{1,0:T(8,128)(2,1)} %w.1, f32[1,100]{1,0:T(1,128)} %bitcast.9, f32[100,768]{1,0:T(8,128)} %tgt_hbm.1, f32[6,128]{1,0:T(8,128)} %bitcast.8, f32[1,100]{1,0:T(1,128)} %bitcast.10), custom_call_target="tpu_custom_call" | custom-call | flops 314572800 | bytes 1572864 | tf_op jit(solution)/shard_map/pallas_call | solution.py:467
  58.4 3.2 %shard_map.94 = (f32[1,1]{1,0:T(1,128)}, bf16[768,1024]{1,0:T(8,128)(2,1)}, f32[100,1024]{1,0:T(8,128)}, f32[1,100]{1,0:T(1,128)}) custom-call(bf16[100,768]{1,0:T(8,128)(2,1)} %get-tuple-element.11.gp, bf16[100,1024]{1,0:T(8,128)(2,1)} %w.1, bf16[50,16,128]{2,1,0:T(8,128)(2,1)} %get-tuple-element.12.f, f32[1,128]{1,0:T(1,128)} %get-tuple-element.13.x), custom_call_target="tpu_custom_call" | custom-call | flops 157286400 | bytes 1572864 | tf_op jit(solution)/shard_map/pallas_call | solution.py:524

commit v5 on v4

--- a/solution.py
+++ b/solution.py
@@ -29,7 +29,7 @@
         self.TAIL = self.T - self.E
         self.STEP = max(1, self.NZ // max(1, self.TAIL))
         self.PL = XL * self.NG
-        nw = min(2, self.VG)
+        nw = min(3, self.VG)
         cuts = [self.VG * i // nw for i in range(nw + 1)]
         self.WAVES = tuple(zip(cuts[:-1], cuts[1:]))
         self.RW = -(-(self.REM * self.HC) // 16)

time: 61.7 us -> 61.7 us (level)
  no operation moved by 1% of the time
where the time goes in v5:
time: 61.7 us; the launch traced here: 61.6 us
  Pallas kernels  60.9 us (99%)
  between operations  0.64 us (1%)
    pallas_call x1, Pallas kernels, body(): pl.pallas_call(functools.partial(kernel, pn), out_shape=(jax.ShapeDtypeSt...  57.7 us
    pallas_call x1, Pallas kernels, body(): pl.pallas_call(functools.partial(finish_kernel, pn), out_shape=(jax.Shape...  3.18 us

profile of v5, /device:TPU:1, one launch (start us, length us, event | category | flops | bytes accessed | tf_op | source)
XLA Modules:
  0.0 61.6 jit_solution(14959886889653496380)
XLA Ops:
  0.6 57.7 %shard_map.93 = (bf16[100,768]{1,0:T(8,128)(2,1)}, bf16[50,16,128]{2,1,0:T(8,128)(2,1)}, f32[1,128]{1,0:T(1,128)}) custom-call(bf16[768,1024]{1,0:T(8,128)(2,1)} %bitcast.7, bf16[100,1024]{1,0:T(8,128)(2,1)} %w.1, f32[1,100]{1,0:T(1,128)} %bitcast.9, f32[100,768]{1,0:T(8,128)} %tgt_hbm.1, f32[6,128]{1,0:T(8,128)} %bitcast.8, f32[1,100]{1,0:T(1,128)} %bitcast.10), custom_call_target="tpu_custom_call" | custom-call | flops 314572800 | bytes 1572864 | tf_op jit(solution)/shard_map/pallas_call | solution.py:467
  58.4 3.2 %shard_map.94 = (f32[1,1]{1,0:T(1,128)}, bf16[768,1024]{1,0:T(8,128)(2,1)}, f32[100,1024]{1,0:T(8,128)}, f32[1,100]{1,0:T(1,128)}) custom-call(bf16[100,768]{1,0:T(8,128)(2,1)} %get-tuple-element.11.gp, bf16[100,1024]{1,0:T(8,128)(2,1)} %w.1, bf16[50,16,128]{2,1,0:T(8,128)(2,1)} %get-tuple-element.12.f, f32[1,128]{1,0:T(1,128)} %get-tuple-element.13.x), custom_call_target="tpu_custom_call" | custom-call | flops 157286400 | bytes 1572864 | tf_op jit(solution)/shard_map/pallas_call | solution.py:524
